TPU v7x, 32 devices: a whole 2x2x4 slice. The times are simulated.
32 devices in a mesh: dp: 8 (over z, x), walk: 4 (over y, core).
Axes of the slice: x: 2, y: 2, z: 4, core: 2. Of those that a mesh axis runs over, the one named last changes fastest.
Arguments:
- fields: float32 [512, 65536], P('walk', 'dp'), may hold values from -6 to 6
- sensitivity: bfloat16 [256, 16, 128, 128], P('dp'), may hold values from -0.125 to 0.125
- tile_index: int32 [256, 16], P('dp'), may hold values from 0 to 511
- tile_count: int32 [256], P('dp'), may hold values from 1 to 16, as said below
- observed: float32 [32768], P('dp'), may hold values from -6 to 6
- precision: float32 [32768], P('dp'), may hold values from 0.2 to 4
Outputs:
- fields_next: float32 [512, 65536], P('walk', 'dp')
Inputs may be any that keep to these rules, and one draw needn't show every extreme that they name: `tile_count`: every block of rows uses between 1 and 16 slots, and some block uses all 16; slots at or past the count are ignored.
All inputs are finite; a program needn't handle non-finite values.
Results may differ from a plain program's by a relative error of at most 0.0023.
Values may be sent and summed in bfloat16 or wider, within the bound.
A program may use at most 128 MiB of HBM per device.

v0:
```python
import jax
import jax.numpy as jnp
from jax import lax
from jax.sharding import PartitionSpec as P

WALKERS = 512


def forward(gathered, sensitivity, tile_index, tile_count):
    walkers_here = gathered.shape[0]
    nblocks = sensitivity.shape[0]
    tile_rows = sensitivity.shape[2]
    cell_blocks = gathered.reshape(walkers_here, -1, tile_rows)
    most_live = jnp.max(tile_count)

    def one_slot(slot_id, totals):
        columns = lax.dynamic_index_in_dim(tile_index, slot_id, 1, keepdims=False)
        blocks = jnp.take(cell_blocks, columns, axis=1)
        sensitive = lax.dynamic_index_in_dim(sensitivity, slot_id, 1, keepdims=False)
        product = jnp.einsum("brc,wbc->wbr", sensitive, blocks, preferred_element_type=jnp.float32)
        alive_mask = (slot_id < tile_count)[None, :, None]
        return totals + jnp.where(alive_mask, product, jnp.float32(0.0))

    start_sum = jnp.zeros((walkers_here, nblocks, tile_rows), jnp.float32)
    totals = lax.fori_loop(0, most_live, one_slot, start_sum)
    return totals.reshape(walkers_here, nblocks * tile_rows)


def local(fields, sensitivity, tile_index, tile_count, observed, precision):
    field_bf = fields.astype(jnp.bfloat16)
    gathered = lax.all_gather(field_bf, "dp", axis=1, tiled=True)
    predicted = forward(gathered, sensitivity, tile_index, tile_count)
    pred_sum = lax.psum(jnp.sum(predicted, axis=0), "walk")
    pred_mean = pred_sum / WALKERS
    deviation = (predicted - pred_mean[None, :]).astype(jnp.bfloat16)
    misfit = (precision[None, :] * (predicted - observed[None, :])).astype(jnp.bfloat16)
    partial_rows = lax.dot_general(
        misfit,
        lax.all_gather(deviation, "walk", axis=0, tiled=True),
        (((1,), (1,)), ((), ())),
        preferred_element_type=jnp.float32,
    )
    coupling_mine = lax.psum(partial_rows, "dp") / WALKERS
    squares = lax.psum(jnp.sum(coupling_mine * coupling_mine), "walk")
    spread = jnp.sqrt(squares / (WALKERS * WALKERS) + 1e-06)
    weights = (8.0 * coupling_mine / (WALKERS * spread)).astype(jnp.bfloat16)
    update = jnp.dot(
        weights,
        lax.all_gather(field_bf, "walk", axis=0, tiled=True),
        preferred_element_type=jnp.float32,
    )
    return fields - update


def solution(mesh):
    placed = (P("walk", "dp"), P("dp", None, None, None), P("dp", None), P("dp"), P("dp"), P("dp"))
    return jax.shard_map(
        local, mesh=mesh, in_specs=placed, out_specs=P("walk", "dp"), check_vma=False
    )
```

profile of v0, /device:TPU:0, one launch (start us, length us, event | category | flops | bytes accessed | tf_op | source)
XLA Modules:
  0.0 632.2 jit_solution(5999888927857076047)
XLA Ops:
  11.9 229.7 %all-gather.4.cloned.1.call-done = bf16[128,65536]{0,1:T(8,128)(2,1)} async-done(((bf16[128,8192]{0,1:T(8,128)(2,1)}), bf16[128,65536]{0,1:T(8,128)(2,1)}) %all-gather.4.cloned.1.call-update) | async-done | bytes 16777232 | tf_op jit(solution)/shard_map/all_gather | solution.py:31
  241.7 22.4 %copy.12 = bf16[128,512,128]{2,0,1:T(8,128)(2,1)} copy(bf16[128,512,128]{0,2,1:T(8,128)(2,1)} %bitcast.37) | data formatting | bytes 33554432 | tf_op jit(solution)/shard_map/while | solution.py:25
  264.3 167.2 %while.10 = (s32[]{:T(128)}, f32[128,32,128]{2,0,1:T(8,128)S(1)}, s32[]{:T(128)}, s32[32]{0:T(128)S(1)}, s32[32,16]{0,1:T(8,128)}, /*index=5*/bf16[128,512,128]{...) while((s32[]{:T(128)}, f32[128,32,128]{2,0,1:T(8,128)S(1)}, ...), condition=%wide.region_2.3_spmd, body=%wide.region_1.2_spmd.sunk | while | flops 135791840 | bytes 8393619 | solution.py:25
  265.6 6.5 %gather_fusion = bf16[32,128,128]{2,1,0:T(8,128)(2,1)S(1)} fusion(bf16[128,512,128]{2,0,1:T(8,128)(2,1)} %get-tuple-element.156, s32[1024]{0:T(1024)S(1)} %pad_clamp_fusion.2), kind=kCustom, calls=%fused_computation.clone.1 | custom fusion | bytes 2097280 | tf_op jit(solution)/shard_map/while/body/jit(_take)/gather | solution.py:18
  276.1 6.5 %gather_fusion = bf16[32,128,128]{2,1,0:T(8,128)(2,1)S(1)} fusion(bf16[128,512,128]{2,0,1:T(8,128)(2,1)} %get-tuple-element.156, s32[1024]{0:T(1024)S(1)} %pad_clamp_fusion.2), kind=kCustom, calls=%fused_computation.clone.1 | custom fusion | bytes 2097280 | tf_op jit(solution)/shard_map/while/body/jit(_take)/gather | solution.py:18
  286.5 6.5 %gather_fusion = bf16[32,128,128]{2,1,0:T(8,128)(2,1)S(1)} fusion(bf16[128,512,128]{2,0,1:T(8,128)(2,1)} %get-tuple-element.156, s32[1024]{0:T(1024)S(1)} %pad_clamp_fusion.2), kind=kCustom, calls=%fused_computation.clone.1 | custom fusion | bytes 2097280 | tf_op jit(solution)/shard_map/while/body/jit(_take)/gather | solution.py:18
  296.9 6.5 %gather_fusion = bf16[32,128,128]{2,1,0:T(8,128)(2,1)S(1)} fusion(bf16[128,512,128]{2,0,1:T(8,128)(2,1)} %get-tuple-element.156, s32[1024]{0:T(1024)S(1)} %pad_clamp_fusion.2), kind=kCustom, calls=%fused_computation.clone.1 | custom fusion | bytes 2097280 | tf_op jit(solution)/shard_map/while/body/jit(_take)/gather | solution.py:18
  307.3 6.5 %gather_fusion = bf16[32,128,128]{2,1,0:T(8,128)(2,1)S(1)} fusion(bf16[128,512,128]{2,0,1:T(8,128)(2,1)} %get-tuple-element.156, s32[1024]{0:T(1024)S(1)} %pad_clamp_fusion.2), kind=kCustom, calls=%fused_computation.clone.1 | custom fusion | bytes 2097280 | tf_op jit(solution)/shard_map/while/body/jit(_take)/gather | solution.py:18
  317.7 6.5 %gather_fusion = bf16[32,128,128]{2,1,0:T(8,128)(2,1)S(1)} fusion(bf16[128,512,128]{2,0,1:T(8,128)(2,1)} %get-tuple-element.156, s32[1024]{0:T(1024)S(1)} %pad_clamp_fusion.2), kind=kCustom, calls=%fused_computation.clone.1 | custom fusion | bytes 2097280 | tf_op jit(solution)/shard_map/while/body/jit(_take)/gather | solution.py:18
  328.1 6.5 %gather_fusion = bf16[32,128,128]{2,1,0:T(8,128)(2,1)S(1)} fusion(bf16[128,512,128]{2,0,1:T(8,128)(2,1)} %get-tuple-element.156, s32[1024]{0:T(1024)S(1)} %pad_clamp_fusion.2), kind=kCustom, calls=%fused_computation.clone.1 | custom fusion | bytes 2097280 | tf_op jit(solution)/shard_map/while/body/jit(_take)/gather | solution.py:18
  338.5 6.5 %gather_fusion = bf16[32,128,128]{2,1,0:T(8,128)(2,1)S(1)} fusion(bf16[128,512,128]{2,0,1:T(8,128)(2,1)} %get-tuple-element.156, s32[1024]{0:T(1024)S(1)} %pad_clamp_fusion.2), kind=kCustom, calls=%fused_computation.clone.1 | custom fusion | bytes 2097280 | tf_op jit(solution)/shard_map/while/body/jit(_take)/gather | solution.py:18
  348.9 6.5 %gather_fusion = bf16[32,128,128]{2,1,0:T(8,128)(2,1)S(1)} fusion(bf16[128,512,128]{2,0,1:T(8,128)(2,1)} %get-tuple-element.156, s32[1024]{0:T(1024)S(1)} %pad_clamp_fusion.2), kind=kCustom, calls=%fused_computation.clone.1 | custom fusion | bytes 2097280 | tf_op jit(solution)/shard_map/while/body/jit(_take)/gather | solution.py:18
  359.3 6.5 %gather_fusion = bf16[32,128,128]{2,1,0:T(8,128)(2,1)S(1)} fusion(bf16[128,512,128]{2,0,1:T(8,128)(2,1)} %get-tuple-element.156, s32[1024]{0:T(1024)S(1)} %pad_clamp_fusion.2), kind=kCustom, calls=%fused_computation.clone.1 | custom fusion | bytes 2097280 | tf_op jit(solution)/shard_map/while/body/jit(_take)/gather | solution.py:18
  369.7 6.5 %gather_fusion = bf16[32,128,128]{2,1,0:T(8,128)(2,1)S(1)} fusion(bf16[128,512,128]{2,0,1:T(8,128)(2,1)} %get-tuple-element.156, s32[1024]{0:T(1024)S(1)} %pad_clamp_fusion.2), kind=kCustom, calls=%fused_computation.clone.1 | custom fusion | bytes 2097280 | tf_op jit(solution)/shard_map/while/body/jit(_take)/gather | solution.py:18
  380.1 6.5 %gather_fusion = bf16[32,128,128]{2,1,0:T(8,128)(2,1)S(1)} fusion(bf16[128,512,128]{2,0,1:T(8,128)(2,1)} %get-tuple-element.156, s32[1024]{0:T(1024)S(1)} %pad_clamp_fusion.2), kind=kCustom, calls=%fused_computation.clone.1 | custom fusion | bytes 2097280 | tf_op jit(solution)/shard_map/while/body/jit(_take)/gather | solution.py:18
  390.5 6.5 %gather_fusion = bf16[32,128,128]{2,1,0:T(8,128)(2,1)S(1)} fusion(bf16[128,512,128]{2,0,1:T(8,128)(2,1)} %get-tuple-element.156, s32[1024]{0:T(1024)S(1)} %pad_clamp_fusion.2), kind=kCustom, calls=%fused_computation.clone.1 | custom fusion | bytes 2097280 | tf_op jit(solution)/shard_map/while/body/jit(_take)/gather | solution.py:18
  401.0 6.5 %gather_fusion = bf16[32,128,128]{2,1,0:T(8,128)(2,1)S(1)} fusion(bf16[128,512,128]{2,0,1:T(8,128)(2,1)} %get-tuple-element.156, s32[1024]{0:T(1024)S(1)} %pad_clamp_fusion.2), kind=kCustom, calls=%fused_computation.clone.1 | custom fusion | bytes 2097280 | tf_op jit(solution)/shard_map/while/body/jit(_take)/gather | solution.py:18
  411.4 6.5 %gather_fusion = bf16[32,128,128]{2,1,0:T(8,128)(2,1)S(1)} fusion(bf16[128,512,128]{2,0,1:T(8,128)(2,1)} %get-tuple-element.156, s32[1024]{0:T(1024)S(1)} %pad_clamp_fusion.2), kind=kCustom, calls=%fused_computation.clone.1 | custom fusion | bytes 2097280 | tf_op jit(solution)/shard_map/while/body/jit(_take)/gather | solution.py:18
  421.8 6.5 %gather_fusion = bf16[32,128,128]{2,1,0:T(8,128)(2,1)S(1)} fusion(bf16[128,512,128]{2,0,1:T(8,128)(2,1)} %get-tuple-element.156, s32[1024]{0:T(1024)S(1)} %pad_clamp_fusion.2), kind=kCustom, calls=%fused_computation.clone.1 | custom fusion | bytes 2097280 | tf_op jit(solution)/shard_map/while/body/jit(_take)/gather | solution.py:18
  433.5 10.5 %psum.21 = f32[4096]{0:T(1024)S(1)} all-reduce(f32[4096]{0:T(1024)S(1)} %bitcast.38), channel_id=1, replica_groups=mesh['dp'=8,'walk'=4] {'walk'}, use_global_device_ids=true, to_apply=%region_4.5 | all-reduce | flops 4096 | bytes 32768 | tf_op jit(solution)/shard_map/psum | solution.py:33
  448.5 33.1 %all-gather.6.cloned.1.call-done = bf16[512,4096]{0,1:T(8,128)(2,1)} async-done(((bf16[128,4096]{0,1:T(8,128)(2,1)}), bf16[512,4096]{0,1:T(8,128)(2,1)}) %all-gather.6.cloned.1.call-update) | async-done | bytes 4194320 | tf_op jit(solution)/shard_map/all_gather | solution.py:39
  485.8 70.1 %all-reduce.2.cloned.1.call-done = f32[128,512]{1,0:T(8,128)} async-done(((f32[128,512]{1,0:T(8,128)}), f32[128,512]{1,0:T(8,128)}) %all-reduce.2.cloned.1.call-update) | async-done | bytes 262160 | tf_op jit(solution)/shard_map/psum | solution.py:43
  564.5 51.7 %all-gather.8.cloned.1.call-done = bf16[512,8192]{0,1:T(8,128)(2,1)} async-done(((bf16[128,8192]{0,1:T(8,128)(2,1)}), bf16[512,8192]{0,1:T(8,128)(2,1)}) %all-gather.8.cloned.1.call-update) | async-done | bytes 8388624 | tf_op jit(solution)/shard_map/all_gather | solution.py:49
  616.2 9.5 %convolution_subtract_fusion = f32[128,8192]{1,0:T(8,128)} fusion(f32[128,8192]{1,0:T(8,128)} %param.8, bf16[512,8192]{0,1:T(8,128)(2,1)} %all-gather.8.cloned.1.call-done, f32[128,512]{1,0:T(8,128)} %all-reduce.2.cloned.1.call-done, f32[]{:T(128)S(6)} %mul.25), kind=kOutput, calls=%fused_computation.14 | convolution fusion | flops 1074987008 | bytes 17039364 | tf_op jit(solution)/shard_map/dot_general | solution.py:47
  (88 shorter events, 76.1 us)
Async XLA Ops:
  6.5 4.7 copy-start.2
  6.5 235.1 %all-gather.4.cloned.1.call-start = ((), (), s32[]{:S(2)}) async-start(), calls=%async_computation | async-start | bytes 18874368 | tf_op jit(solution)/shard_map/all_gather | solution.py:31
  11.2 470.4 %all-gather.6.cloned.1.call-start = ((), (), s32[]{:S(2)}) async-start(), calls=%async_computation.1 | async-start | bytes 5242880 | tf_op jit(solution)/shard_map/all_gather | solution.py:39
  431.5 12.5 %copy-start = (f32[4096]{0:T(1024)S(1)}, f32[4096]{0:T(1024)}, u32[]{:S(2)}) copy-start(f32[4096]{0:T(1024)} %param.12) | copy-start | bytes 49156
  431.5 12.5 %copy-start.1 = (f32[4096]{0:T(1024)S(1)}, f32[4096]{0:T(1024)}, u32[]{:S(2)}) copy-start(f32[4096]{0:T(1024)} %param.13) | copy-start | bytes 49156
  448.5 107.5 %all-reduce.2.cloned.1.call-start = ((), (), s32[]{:S(2)}) async-start(), calls=%async_computation.2 | async-start | bytes 524288 | tf_op jit(solution)/shard_map/psum | solution.py:43
  485.3 130.9 %all-gather.8.cloned.1.call-start = ((), (), s32[]{:S(2)}) async-start(), calls=%async_computation.3 | async-start | bytes 10485760 | tf_op jit(solution)/shard_map/all_gather | solution.py:49
Sparse Core Ops, SparseCore 0:
  11.3 230.2 all-gather.3
  448.6 32.9 all-gather.5
  485.4 70.5 all-reduce.1
  557.5 58.6 all-gather.7
where the time goes:
time: 635 us; the launch traced here: 632 us
  waiting for transfers between devices  385 us (61%)
  local copies, waits for them, and re-layouts  133 us (21%)
  matrix products  53.6 us (8%)
  other arithmetic  18.3 us (3%)
  blocking collectives  16.7 us (3%)
  between operations  13.8 us (2%)
  loops' own time  11 us (2%)
    all_gather x1, waiting for transfers between devices, local(): gathered = lax.all_gather(field_bf, 'dp', axis=1, tiled=True)  230 us
    gather x16, local copies, waits for them, and re-layouts, one_slot(): blocks = jnp.take(cell_blocks, columns, axis=1)  104 us
    psum x1, waiting for transfers between devices, local(): coupling_mine = lax.psum(partial_rows, 'dp') / WALKERS  70.1 us
    all_gather x1, waiting for transfers between devices, local(): lax.all_gather(field_bf, 'walk', axis=0, tiled=True)  51.7 us
    dot_general x16, matrix products, one_slot(): jnp.einsum('brc,wbc->wbr', sensitive, blocks, preferred_element_type=jnp....  40.4 us
    all_gather x1, waiting for transfers between devices, local(): lax.all_gather(deviation, 'walk', axis=0, tiled=True)  33.1 us
    while x2, local copies, waits for them, and re-layouts, forward(): totals = lax.fori_loop(0, most_live, one_slot, start_sum)  24.3 us
  transfers between devices with their start and end apart: 4, of which 4 were waited for; matrix products, arithmetic and copies ran while one was open for 0% of the time, Pallas kernels for 0%

commit v1 on v0

--- a/solution.py
+++ b/solution.py
@@ -4,6 +4,22 @@
 from jax.sharding import PartitionSpec as P
 
 WALKERS = 512
+
+
+def ring_gather(x, axis, dim):
+    ways, here, hop = (lax.axis_size(axis), lax.axis_index(axis), x.shape[dim])
+    shape = [n * ways if d == dim else n for d, n in enumerate(x.shape)]
+    full = lax.dynamic_update_slice_in_dim(jnp.zeros(shape, x.dtype), x, here * hop, axis=dim)
+    going_up = going_down = x
+    for far in range(1, ways // 2 + 1):
+        going_up = lax.ppermute(going_up, axis, [(d, (d + 1) % ways) for d in range(ways)])
+        full = lax.dynamic_update_slice_in_dim(full, going_up, (here - far) % ways * hop, axis=dim)
+        if 2 * far < ways:
+            going_down = lax.ppermute(going_down, axis, [(d, (d - 1) % ways) for d in range(ways)])
+            full = lax.dynamic_update_slice_in_dim(
+                full, going_down, (here + far) % ways * hop, axis=dim
+            )
+    return full
 
 
 def forward(gathered, sensitivity, tile_index, tile_count):
@@ -28,7 +44,7 @@
 
 def local(fields, sensitivity, tile_index, tile_count, observed, precision):
     field_bf = fields.astype(jnp.bfloat16)
-    gathered = lax.all_gather(field_bf, "dp", axis=1, tiled=True)
+    gathered = ring_gather(field_bf, "dp", 1)
     predicted = forward(gathered, sensitivity, tile_index, tile_count)
     pred_sum = lax.psum(jnp.sum(predicted, axis=0), "walk")
     pred_mean = pred_sum / WALKERS

time: 635 us -> 729 us (1.15)
  waiting for transfers between devices: 385 us -> 436 us
  local copies, waits for them, and re-layouts: 133 us -> 157 us
  starting transfers between devices: 0.13 us -> 19.8 us
    ppermute x0 -> x7, waiting for transfers between devices: none -> 283 us  [the longest x4 241 us: ring_gather(): lax.ppermute(going_up, axis, [(d, (d + 1) % ways) for d in range(ways)])]
    all_gather x1 -> x0, waiting for transfers between devices: 230 us -> none  [local(): gathered = lax.all_gather(field_bf, 'dp', axis=1, tiled=True)]
    ppermute x0 -> x7, starting transfers between devices: none -> 19.7 us  [the longest x4 10.4 us: ring_gather(): lax.ppermute(going_up, axis, [(d, (d + 1) % ways) for d in range(ways)])]
    dynamic_update_slice x0 -> x8, local copies, waits for them, and re-layouts: none -> 18.1 us  [the longest x4 9.04 us: ring_gather(): lax.dynamic_update_slice_in_dim(full, going_up, (here - far) % ways * hop...]
  transfers between devices with their start and end apart: 4 -> 10, of which waited for: 4 -> 7; matrix products, arithmetic and copies ran while one was open for 0% -> 3% of each run, Pallas kernels for 0% -> 0%
where the time goes in v1:
time: 729 us; the launch traced here: 726 us
  waiting for transfers between devices  436 us (60%)
  local copies, waits for them, and re-layouts  157 us (22%)
  matrix products  53.6 us (7%)
  starting transfers between devices  19.8 us (3%)
  other arithmetic  18.3 us (3%)
  blocking collectives  17.5 us (2%)
  between operations  13.9 us (2%)
  loops' own time  9.94 us (1%)
    ppermute x4, waiting for transfers between devices, ring_gather(): lax.ppermute(going_up, axis, [(d, (d + 1) % ways) for d in range(ways)])  241 us
    gather x16, local copies, waits for them, and re-layouts, one_slot(): blocks = jnp.take(cell_blocks, columns, axis=1)  104 us
    psum x1, waiting for transfers between devices, local(): coupling_mine = lax.psum(partial_rows, 'dp') / WALKERS  70 us
    all_gather x1, waiting for transfers between devices, local(): lax.all_gather(field_bf, 'walk', axis=0, tiled=True)  51.6 us
    ppermute x3, waiting for transfers between devices, ring_gather(): lax.ppermute(going_down, axis, [(d, (d - 1) % ways) for d in range(ways)])  41.5 us
    dot_general x16, matrix products, one_slot(): jnp.einsum('brc,wbc->wbr', sensitive, blocks, preferred_element_type=jnp....  40.5 us
    all_gather x1, waiting for transfers between devices, local(): lax.all_gather(deviation, 'walk', axis=0, tiled=True)  31.4 us
    while x2, local copies, waits for them, and re-layouts, forward(): totals = lax.fori_loop(0, most_live, one_slot, start_sum)  24.2 us
  transfers between devices with their start and end apart: 10, of which 7 were waited for; matrix products, arithmetic and copies ran while one was open for 3% of the time, Pallas kernels for 0%

profile of v1, /device:TPU:0, one launch (start us, length us, event | category | flops | bytes accessed | tf_op | source)
XLA Modules:
  0.0 726.0 jit_solution(16193383449347906237)
XLA Ops:
  16.3 86.7 %collective-permute-done = bf16[128,8192]{0,1:T(8,128)(2,1)} collective-permute-done((bf16[128,8192]{0,1:T(8,128)(2,1)S(1)}, bf16[128,8192]{0,1:T(8,128)(2,1)}, u32[]{:S(2)}, u32[]{:S(2)}) %collective-permute-start) | collective-permute-done | bytes 2097184 | tf_op jit(solution)/shard_map/ppermute | solution.py:15
  116.8 78.2 %collective-permute-done.2 = bf16[128,8192]{0,1:T(8,128)(2,1)} collective-permute-done((bf16[128,8192]{0,1:T(8,128)(2,1)}, bf16[128,8192]{0,1:T(8,128)(2,1)}, u32[]{:S(2)}, u32[]{:S(2)}) %collective-permute-start.2) | collective-permute-done | bytes 2097184 | tf_op jit(solution)/shard_map/ppermute | solution.py:15
  209.6 76.3 %collective-permute-done.4 = bf16[128,8192]{0,1:T(8,128)(2,1)S(1)} collective-permute-done((bf16[128,8192]{0,1:T(8,128)(2,1)}, bf16[128,8192]{0,1:T(8,128)(2,1)S(1)}, u32[]{:S(2)}, u32[]{:S(2)}) %collective-permute-start.4) | collective-permute-done | bytes 2097184 | tf_op jit(solution)/shard_map/ppermute | solution.py:15
  292.9 41.5 %collective-permute-done.5 = bf16[128,8192]{0,1:T(8,128)(2,1)S(1)} collective-permute-done((bf16[128,8192]{0,1:T(8,128)(2,1)}, bf16[128,8192]{0,1:T(8,128)(2,1)S(1)}, u32[]{:S(2)}, u32[]{:S(2)}) %collective-permute-start.5) | collective-permute-done | bytes 2097184 | tf_op jit(solution)/shard_map/ppermute | solution.py:18
  337.4 22.4 %copy.12 = bf16[128,512,128]{2,0,1:T(8,128)(2,1)} copy(bf16[128,512,128]{0,2,1:T(8,128)(2,1)} %bitcast.5) | data formatting | bytes 33554432 | tf_op jit(solution)/shard_map/while | solution.py:41
  360.0 166.1 %while.10 = (s32[]{:T(128)}, f32[128,32,128]{2,0,1:T(8,128)S(1)}, s32[]{:T(128)}, s32[32]{0:T(128)S(1)}, s32[32,16]{0,1:T(8,128)}, /*index=5*/bf16[128,512,128]{...) while((s32[]{:T(128)}, f32[128,32,128]{2,0,1:T(8,128)S(1)}, ...), condition=%wide.region_2.3_spmd, body=%wide.region_1.2_spmd.sunk | while | flops 135791840 | bytes 8393619 | solution.py:41
  361.2 6.5 gather_fusion
  371.6 6.5 gather_fusion
  381.9 6.5 gather_fusion
  392.3 6.5 gather_fusion
  402.6 6.5 gather_fusion
  423.3 6.5 gather_fusion
  433.7 6.5 gather_fusion
  444.0 6.5 gather_fusion
  454.4 6.5 gather_fusion
  464.7 6.5 gather_fusion
  475.1 6.5 gather_fusion
  495.8 6.5 gather_fusion
  506.1 6.5 gather_fusion
  528.1 11.2 %psum.21 = f32[4096]{0:T(1024)S(1)} all-reduce(f32[4096]{0:T(1024)S(1)} %bitcast.37), channel_id=1, replica_groups=mesh['dp'=8,'walk'=4] {'walk'}, use_global_device_ids=true, to_apply=%region_4.5 | all-reduce | flops 4096 | bytes 32768 | tf_op jit(solution)/shard_map/psum | solution.py:49
  543.9 31.4 %all-gather.3.cloned.1.call-done = bf16[512,4096]{0,1:T(8,128)(2,1)} async-done(((bf16[128,4096]{0,1:T(8,128)(2,1)}), bf16[512,4096]{0,1:T(8,128)(2,1)}) %all-gather.3.cloned.1.call-update) | async-done | bytes 4194320 | tf_op jit(solution)/shard_map/all_gather | solution.py:55
  579.7 70.0 %all-reduce.2.cloned.1.call-done = f32[128,512]{1,0:T(8,128)} async-done(((f32[128,512]{1,0:T(8,128)}), f32[128,512]{1,0:T(8,128)}) %all-reduce.2.cloned.1.call-update) | async-done | bytes 262160 | tf_op jit(solution)/shard_map/psum | solution.py:59
  658.4 51.6 %all-gather.5.cloned.1.call-done = bf16[512,8192]{0,1:T(8,128)(2,1)} async-done(((bf16[128,8192]{0,1:T(8,128)(2,1)}), bf16[512,8192]{0,1:T(8,128)(2,1)}) %all-gather.5.cloned.1.call-update) | async-done | bytes 8388624 | tf_op jit(solution)/shard_map/all_gather | solution.py:65
  710.0 9.5 %convolution_subtract_fusion = f32[128,8192]{1,0:T(8,128)} fusion(f32[128,8192]{1,0:T(8,128)} %param.8, bf16[512,8192]{0,1:T(8,128)(2,1)} %all-gather.5.cloned.1.call-done, f32[128,512]{1,0:T(8,128)} %all-reduce.2.cloned.1.call-done, f32[]{:T(128)S(6)} %mul.57), kind=kOutput, calls=%fused_computation.14 | convolution fusion | flops 1074987008 | bytes 17039364 | tf_op jit(solution)/shard_map/dot_general | solution.py:63
  (110 shorter events, 138.7 us)
Async XLA Ops:
  6.5 568.8 %all-gather.3.cloned.1.call-start = ((), (), s32[]{:S(2)}) async-start(), calls=%async_computation | async-start | bytes 5242880 | tf_op jit(solution)/shard_map/all_gather | solution.py:55
  10.2 104.5 %copy-start = (bf16[128,8192]{0,1:T(8,128)(2,1)}, bf16[128,8192]{0,1:T(8,128)(2,1)S(1)}, u32[]{:S(2)}) copy-start(bf16[128,8192]{0,1:T(8,128)(2,1)S(1)} %copy.11) | copy-start | bytes 6291460
  10.3 92.8 %collective-permute-start = (bf16[128,8192]{0,1:T(8,128)(2,1)S(1)}, bf16[128,8192]{0,1:T(8,128)(2,1)}, u32[]{:S(2)}, u32[]{:S(2)}) collective-permute-start(bf16[128,8192]{0,1:T(8,128)(2,1)S(1)} %copy.11), channel_id=1, source_target_pairs={{0,4},{4,8},{8,12},{12,16},{16,20},{20,24},{24,28},{28,0},{1,5},{5... | collective-permute-start | bytes 6291464 | tf_op jit(solution)/shard_map/ppermute | solution.py:15
  13.2 92.4 %collective-permute-start.1 = (bf16[128,8192]{0,1:T(8,128)(2,1)S(1)}, bf16[128,8192]{0,1:T(8,128)(2,1)}, u32[]{:S(2)}, u32[]{:S(2)}) collective-permute-start(bf16[128,8192]{0,1:T(8,128)(2,1)S(1)} %copy.11), channel_id=1, source_target_pairs={{0,28},{4,0},{8,4},{12,8},{16,12},{20,16},{24,20},{28,24},{1,29},{... | collective-permute-start | bytes 6291464 | tf_op jit(solution)/shard_map/ppermute | solution.py:18
  103.1 91.9 %collective-permute-start.2 = (bf16[128,8192]{0,1:T(8,128)(2,1)}, bf16[128,8192]{0,1:T(8,128)(2,1)}, u32[]{:S(2)}, u32[]{:S(2)}) collective-permute-start(bf16[128,8192]{0,1:T(8,128)(2,1)} %collective-permute-done), channel_id=1, source_target_pairs={{0,4},{4,8},{8,12},{12,16},{16,20},{20,24},{24,28},{28,0},{1,5},{5... | collective-permute-start | bytes 6291464 | tf_op jit(solution)/shard_map/ppermute | solution.py:15
  105.7 97.8 %collective-permute-start.3 = (bf16[128,8192]{0,1:T(8,128)(2,1)}, bf16[128,8192]{0,1:T(8,128)(2,1)}, u32[]{:S(2)}, u32[]{:S(2)}) collective-permute-start(bf16[128,8192]{0,1:T(8,128)(2,1)} %collective-permute-done.1), channel_id=1, source_target_pairs={{0,28},{4,0},{8,4},{12,8},{16,12},{20,16},{24,20},{28,24},{1,29},{... | collective-permute-start | bytes 6291464 | tf_op jit(solution)/shard_map/ppermute | solution.py:18
  114.7 1.5 copy-start.3
  194.9 91.1 %collective-permute-start.4 = (bf16[128,8192]{0,1:T(8,128)(2,1)}, bf16[128,8192]{0,1:T(8,128)(2,1)S(1)}, u32[]{:S(2)}, u32[]{:S(2)}) collective-permute-start(bf16[128,8192]{0,1:T(8,128)(2,1)} %collective-permute-done.2), channel_id=1, source_target_pairs={{0,4},{4,8},{8,12},{12,16},{16,20},{20,24},{24,28},{28,0},{1,5},{5... | collective-permute-start | bytes 6291464 | tf_op jit(solution)/shard_map/ppermute | solution.py:15
  203.5 130.9 %collective-permute-start.5 = (bf16[128,8192]{0,1:T(8,128)(2,1)}, bf16[128,8192]{0,1:T(8,128)(2,1)S(1)}, u32[]{:S(2)}, u32[]{:S(2)}) collective-permute-start(bf16[128,8192]{0,1:T(8,128)(2,1)} %collective-permute-done.3), channel_id=1, source_target_pairs={{0,28},{4,0},{8,4},{12,8},{16,12},{20,16},{24,20},{28,24},{1,29},{... | collective-permute-start | bytes 6291464 | tf_op jit(solution)/shard_map/ppermute | solution.py:18
  286.0 49.9 %collective-permute-start.6 = (bf16[128,8192]{0,1:T(8,128)(2,1)S(1)}, bf16[128,8192]{0,1:T(8,128)(2,1)S(1)}, u32[]{:S(2)}, u32[]{:S(2)}) collective-permute-start(bf16[128,8192]{0,1:T(8,128)(2,1)S(1)} %collective-permute-done.4), channel_id=1, source_target_pairs={{0,4},{4,8},{8,12},{12,16},{16,20},{20,24},{24,28},{28,0},{1,5},{5... | collective-permute-start | bytes 6291464 | tf_op jit(solution)/shard_map/ppermute | solution.py:15
  526.1 13.2 %copy-start.1 = (f32[4096]{0:T(1024)S(1)}, f32[4096]{0:T(1024)}, u32[]{:S(2)}) copy-start(f32[4096]{0:T(1024)} %param.12) | copy-start | bytes 49156
  526.1 13.2 %copy-start.2 = (f32[4096]{0:T(1024)S(1)}, f32[4096]{0:T(1024)}, u32[]{:S(2)}) copy-start(f32[4096]{0:T(1024)} %param.13) | copy-start | bytes 49156
  543.8 105.8 %all-reduce.2.cloned.1.call-start = ((), (), s32[]{:S(2)}) async-start(), calls=%async_computation.1 | async-start | bytes 524288 | tf_op jit(solution)/shard_map/psum | solution.py:59
  579.0 131.1 %all-gather.5.cloned.1.call-start = ((), (), s32[]{:S(2)}) async-start(), calls=%async_computation.2 | async-start | bytes 10485760 | tf_op jit(solution)/shard_map/all_gather | solution.py:65
Sparse Core Ops, SparseCore 0:
  544.0 31.2 all-gather.2
  579.1 70.5 all-reduce.1
  651.3 58.6 all-gather.4
